TPU v7x, 1024 devices: a whole 8x8x8 slice. The times are simulated.
1024 devices in a mesh: col: 16 (over x, core), tab: 32 (over z, y_hi), dp: 2 (over y_lo).
Axes of the slice: x: 8, y: 8 (y_hi: 4, y_lo: 2; y = y_hi * 2 + y_lo), z: 8, core: 2. Of those that a mesh axis runs over, the one named last changes fastest.
Arguments:
- wide_rows: bfloat16 [2, 64, 2048, 1024], P(None, ('tab', 'dp'), None, 'col'), may hold values from -6 to 6
- wide_lengths: int32 [2, 64, 512], P(None, ('tab', 'dp')), may hold values from 1 to 12, 2048 in all within a row
- narrow_rows: bfloat16 [32, 32, 4096, 128], P('tab', ('col', 'dp')), may hold values from -6 to 6
- narrow_lengths: int32 [32, 32, 1024], P('tab', ('col', 'dp')), may hold values from 1 to 12, 4096 in all within a row
- narrow_widths: int32 [32], P('tab'), may hold values from 32 to 128
- wide_proj: bfloat16 [2, 1024, 512], P(None, 'col'), may hold values from -0.09375 to 0.09375
- narrow_proj: bfloat16 [32, 128, 512], P('tab'), may hold values from -0.25 to 0.25
- cotangent: bfloat16 [32768, 512], P(('col', 'tab', 'dp')), may hold values from -24 to 24
Outputs:
- cross_input: bfloat16 [32768, 512], P(('col', 'tab', 'dp'))
- wide_row_grads: bfloat16 [2, 64, 2048, 1024], P(None, ('tab', 'dp'), None, 'col')
- narrow_row_grads: bfloat16 [32, 32, 4096, 128], P('tab', ('col', 'dp'))
- wide_proj_grads: float32 [2, 1024, 512], P(None, 'col', ('tab', 'dp'))
- narrow_proj_grads: float32 [32, 128, 512], P('tab', None, ('col', 'dp'))
Inputs may be any that keep to these rules, and one draw needn't show every extreme that they name: `wide_lengths`: in each table and block the lengths sum to the block's rows (2048 for wide tables) and some bag has exactly 12 rows. `narrow_lengths`: in each table and block the lengths sum to 4096 and some bag has exactly 12 rows.
All inputs are finite; a program needn't handle non-finite values.
Results may differ from a plain program's by a relative error of at most 0.0049.
Values may be sent and summed in bfloat16 or wider, within the bound.
A program may use at most 32 MiB of HBM per device.

v0:
```python
import jax
import jax.numpy as jnp
from jax import lax
from jax.sharding import PartitionSpec as P


def bag_mask(lengths, count):
    ends = jnp.cumsum(lengths)
    starts = ends - lengths
    places = jnp.arange(count, dtype=jnp.int32)
    inside = (places[None, :] >= starts[:, None]) & (places[None, :] < ends[:, None])
    return inside.astype(jnp.bfloat16)


def body(
    wide_rows,
    wide_lengths,
    narrow_rows,
    narrow_lengths,
    narrow_widths,
    wide_proj,
    narrow_proj,
    cotangent,
):
    per_device = cotangent.shape[0]
    out_width = cotangent.shape[1]
    wide_count = wide_rows.shape[0]
    narrow_count = narrow_rows.shape[0]
    slot_width = narrow_rows.shape[3]
    tab_count = lax.axis_size("tab")
    factor = (wide_count + narrow_count * tab_count) ** (-0.5)
    wide_masks = jax.vmap(bag_mask, in_axes=(0, None))(wide_lengths[:, 0], wide_rows.shape[2])
    wide_pooled = jnp.einsum(
        "wsr,wrk->wsk", wide_masks, wide_rows[:, 0], preferred_element_type=jnp.float32
    ).astype(jnp.bfloat16)
    narrow_masks = jax.vmap(bag_mask, in_axes=(0, None))(narrow_lengths[:, 0], narrow_rows.shape[2])
    keep = jnp.arange(slot_width, dtype=jnp.int32)[None, :] < narrow_widths[:, None]
    narrow_sum = jnp.einsum(
        "tsr,trk->tsk", narrow_masks, narrow_rows[:, 0], preferred_element_type=jnp.float32
    )
    narrow_pooled = jnp.where(keep[:, None, :], narrow_sum, 0.0).astype(jnp.bfloat16)
    narrow_term = factor * jnp.einsum(
        "tsk,tkd->sd", narrow_pooled, narrow_proj, preferred_element_type=jnp.float32
    )
    arrived = lax.all_to_all(
        narrow_term.reshape(tab_count, per_device, out_width),
        "tab",
        split_axis=0,
        concat_axis=0,
        tiled=True,
    )
    partial_term = factor * jnp.einsum(
        "wsk,wkd->sd", wide_pooled, wide_proj, preferred_element_type=jnp.float32
    )
    summed = lax.psum(partial_term, "col")
    wide_term = lax.dynamic_slice_in_dim(summed, lax.axis_index("col") * per_device, per_device, 0)
    cross_input = (wide_term + jnp.sum(arrived, axis=0)).astype(jnp.bfloat16)
    piece = lax.all_gather(cotangent, "col", axis=0, tiled=True)
    pooled_rows = wide_pooled
    grads = jnp.einsum("wsk,sd->wkd", pooled_rows, piece, preferred_element_type=jnp.float32)
    part = jnp.einsum("sd,wkd->wsk", piece, wide_proj, preferred_element_type=jnp.float32)
    backs = part
    wide_grads = grads
    wide_backs = backs
    wide_backs = (factor * wide_backs).astype(jnp.bfloat16)
    wide_row_grads = jnp.einsum(
        "wsr,wsk->wrk", wide_masks, wide_backs, preferred_element_type=jnp.float32
    ).astype(jnp.bfloat16)[:, None]
    piece = lax.all_gather(cotangent, "tab", axis=0, tiled=True)
    pooled_rows = narrow_pooled
    grads = jnp.einsum("tsk,sd->tkd", pooled_rows, piece, preferred_element_type=jnp.float32)
    part = jnp.einsum("sd,tkd->tsk", piece, narrow_proj, preferred_element_type=jnp.float32)
    backs = part
    narrow_backs = backs
    narrow_backs = jnp.where(keep[:, None, :], factor * narrow_backs, 0.0).astype(jnp.bfloat16)
    narrow_row_grads = jnp.einsum(
        "tsr,tsk->trk", narrow_masks, narrow_backs, preferred_element_type=jnp.float32
    ).astype(jnp.bfloat16)[:, None]
    wide_grads = factor * wide_grads
    total_grads = lax.psum(wide_grads, ("tab", "dp"))
    share = out_width // lax.axis_size(("tab", "dp"))
    wide_proj_grads = lax.dynamic_slice_in_dim(
        total_grads, lax.axis_index(("tab", "dp")) * share, share, 2
    )
    narrow_proj_grads = lax.psum_scatter(
        factor * grads, ("col", "dp"), scatter_dimension=2, tiled=True
    )
    return (cross_input, wide_row_grads, narrow_row_grads, wide_proj_grads, narrow_proj_grads)


def solution(mesh):
    in_specs = (
        P(None, ("tab", "dp"), None, "col"),
        P(None, ("tab", "dp"), None),
        P("tab", ("col", "dp"), None, None),
        P("tab", ("col", "dp"), None),
        P("tab"),
        P(None, "col", None),
        P("tab", None, None),
        P(("col", "tab", "dp"), None),
    )
    out_specs = (
        P(("col", "tab", "dp"), None),
        P(None, ("tab", "dp"), None, "col"),
        P("tab", ("col", "dp"), None, None),
        P(None, "col", ("tab", "dp")),
        P("tab", None, ("col", "dp")),
    )
    return jax.shard_map(body, mesh=mesh, in_specs=in_specs, out_specs=out_specs, check_vma=False)
```

profile of v0, /device:TPU:1, one launch (start us, length us, event | category | flops | bytes accessed | tf_op | source)
XLA Modules:
  0.0 375.0 jit_solution(2881709578806074084)
XLA Ops:
  8.0 1.1 reduce-window.16
  9.1 0.2 slice_reduce_fusion.1
  9.3 0.2 reduce-window.19
  10.1 0.1 broadcast.64
  10.2 0.7 fusion.62
  10.9 4.6 %fusion.38 = bf16[1024,128]{1,0:T(8,128)(2,1)S(1)} fusion(s32[1024]{0:T(1024)S(1)} %get-tuple-element.21, s32[1024]{0:T(1024)S(1)} %get-tuple-element.20, bf16[1,1,4096,128]{3,2,1,0:T(8,128)(2,1)S(1)} %copy-done, pred[128]{0:T(512)(128)(4,1)S(1)} %iota_compare_fusion.4), kind=kOutput, calls=%fused_computation.31 | convolution fusion | flops 1086586880 | bytes 1319040 | tf_op jit(solution)/shard_map/tsr,trk->tsk/dot_general | solution.py:38
  15.5 1.8 convolution_multiply_fusion
  17.3 23.5 %all-to-all-start = ((f32[32,32,512]{2,1,0:T(8,128)}), f32[32,32,512]{2,1,0:T(8,128)S(1)}, u32[]{:S(2)}, u32[]{:S(2)}) async-start(f32[32,32,512]{2,1,0:T(8,128)} %bitcast.78), calls=%async_computation | async-start | bytes 4194304 | tf_op jit(solution)/shard_map/all_to_all | solution.py:45
  40.8 0.0 all-reduce.5.cloned.1.call-start
  40.8 0.6 reduce-window.14
  41.4 0.2 slice_reduce_fusion
  41.7 0.2 reduce-window.15
  41.8 0.1 add_bitcast_fusion
  41.9 3.8 %fusion.44 = bf16[2,512,64]{1,2,0:T(8,128)(2,1)S(1)} fusion(s32[2,512]{1,0:T(2,128)S(1)} %bitcast.84, s32[2,512]{1,0:T(2,128)S(1)} %bitcast_subtract_fusion, bf16[2,1,2048,64]{2,3,1,0:T(8,128)(2,1)} %param.8), kind=kOutput, calls=%fused_computation.38 | convolution fusion | flops 274792448 | bytes 663552 | tf_op jit(solution)/shard_map/wsr,wrk->wsk/dot_general | solution.py:33
  45.8 19.2 %all_gather.6 = bf16[512,512]{1,0:T(8,128)(2,1)S(1)} all-gather(bf16[32,512]{1,0:T(8,128)(2,1)S(1)} %copy-done.4), channel_id=1, replica_groups=mesh['col'=16,'tab'=32,'dp'=2] {'col'}, dimensions={0}, use_global_device_ids=true | all-gather | bytes 557056 | tf_op jit(solution)/shard_map/all_gather | solution.py:58
  65.0 0.8 copy-done.1
  65.8 1.0 convolution_multiply_fusion.2
  66.7 0.0 all-gather.2.cloned.1.call-start
  66.8 0.5 all-gather.2.cloned.1.call-update
  67.3 0.0 all-reduce.3.cloned.1.call-start
  67.4 2.2 fusion.31
  69.6 0.2 reduce-scatter.2.cloned.1.call-start
  69.8 4.7 %fusion.28 = bf16[2,1,2048,64]{2,3,1,0:T(8,128)(2,1)} fusion(s32[2,512]{1,0:T(2,128)S(1)} %bitcast.85, s32[2,512]{1,0:T(2,128)S(1)} %bitcast_subtract_fusion, bf16[2,64,512]{2,1,0:T(8,128)(2,1)} %param.13, bf16[512,512]{1,0:T(8,128)(2,1)} %copy-done.1), kind=kOutput, calls=%fused_computation.22 | convolution fusion | flops 342228992 | bytes 1187840 | tf_op jit(solution)/shard_map/wsr,wsk->wrk/dot_general | solution.py:66
  74.5 166.2 %all-reduce.5.cloned.1.call-done = f32[2,64,512]{2,1,0:T(8,128)} async-done(((f32[2,64,512]{2,1,0:T(8,128)}), f32[2,64,512]{2,1,0:T(8,128)}) %all-reduce.5.cloned.1.call-update) | async-done | bytes 262160 | tf_op jit(solution)/shard_map/psum | solution.py:80
  240.7 0.9 constant_dynamic-slice_fusion
  241.6 0.7 copy.22
  242.3 2.3 fusion.42
  244.6 1.8 copy.20
  246.4 7.1 %fusion.18 = bf16[1,1,4096,128]{3,2,1,0:T(8,128)(2,1)} fusion(s32[1024]{0:T(1024)S(1)} %get-tuple-element.21, s32[1024]{0:T(1024)S(1)} %get-tuple-element.20, bf16[1024,512]{1,0:T(8,128)(2,1)} %all-gather.2.cloned.1.call-done, pred[128]{0:T(512)(128)(4,1)S(1)} %copy-done.7, bf16[1,128,512]{2,1,0:T(8,128)(2,1)S(1)} %copy-done.3), kind=kOutput, calls=%fused_computation.16 | convolution fusion | flops 1225654272 | bytes 2236544 | tf_op jit(solution)/shard_map/tsr,tsk->trk/dot_general | solution.py:76
  253.5 0.1 reduce_sum.9
  253.7 112.4 %all-reduce.3.cloned.1.call-done = f32[512,512]{1,0:T(8,128)} async-done(((f32[512,512]{1,0:T(8,128)}), f32[512,512]{1,0:T(8,128)}) %all-reduce.3.cloned.1.call-update) | async-done | bytes 1048592 | tf_op jit(solution)/shard_map/psum | solution.py:55
  366.1 1.5 add_convert_fusion
  (25 shorter events, 0.1 us)
Async XLA Ops:
  8.0 2.9 copy-start
  10.1 5.4 %copy-start.6 = (pred[128]{0:T(512)(128)(4,1)}, pred[128]{0:T(512)(128)(4,1)S(1)}, u32[]{:S(2)}) copy-start(pred[128]{0:T(512)(128)(4,1)S(1)} %iota_compare_fusion.4) | copy-start | bytes 388
  10.9 4.6 %copy-start.2 = (bf16[1,128,512]{2,1,0:T(8,128)(2,1)S(1)}, bf16[1,128,512]{2,1,0:T(8,128)(2,1)}, u32[]{:S(2)}) copy-start(bf16[1,128,512]{2,1,0:T(8,128)(2,1)} %param.14) | copy-start | bytes 393220
  17.3 23.5 %copy-start.5 = (s32[2,1,512]{2,1,0:T(1,128)S(1)}, s32[2,1,512]{2,1,0:T(1,128)}, u32[]{:S(2)}) copy-start(s32[2,1,512]{2,1,0:T(1,128)} %param.9) | copy-start | bytes 12292
  17.3 236.3 %all-to-all-start = ((f32[32,32,512]{2,1,0:T(8,128)}), f32[32,32,512]{2,1,0:T(8,128)S(1)}, u32[]{:S(2)}, u32[]{:S(2)}) async-start(f32[32,32,512]{2,1,0:T(8,128)} %bitcast.78), calls=%async_computation | async-start | bytes 4194304 | tf_op jit(solution)/shard_map/all_to_all | solution.py:45
  40.8 200.0 %all-reduce.5.cloned.1.call-start = ((), (), s32[]{:S(2)}) async-start(), calls=%async_computation.4 | async-start | bytes 524288 | tf_op jit(solution)/shard_map/psum | solution.py:80
  41.9 3.8 %copy-start.4 = (bf16[32,512]{1,0:T(8,128)(2,1)S(1)}, bf16[32,512]{1,0:T(8,128)(2,1)}, u32[]{:S(2)}) copy-start(bf16[32,512]{1,0:T(8,128)(2,1)} %param.15) | copy-start | bytes 98308
  65.0 0.8 copy-start.1
  66.7 175.6 %all-gather.2.cloned.1.call-start = ((), (), s32[]{:S(2)}) async-start(), calls=%async_computation.3 | async-start | bytes 1081344 | tf_op jit(solution)/shard_map/all_gather | solution.py:69
  67.3 298.8 %all-reduce.3.cloned.1.call-start = ((), (), s32[]{:S(2)}) async-start(), calls=%async_computation.2 | async-start | bytes 2097152 | tf_op jit(solution)/shard_map/psum | solution.py:55
  69.6 298.0 %reduce-scatter.2.cloned.1.call-start = ((), (), s32[]{:S(2)}) async-start(), calls=%async_computation.5 | async-start | bytes 270336 | tf_op jit(solution)/shard_map/reduce_scatter | solution.py:85
  74.5 171.9 %copy-start.7 = (pred[128]{0:T(512)(128)(4,1)S(1)}, pred[128]{0:T(512)(128)(4,1)}, u32[]{:S(2)}) copy-start(pred[128]{0:T(512)(128)(4,1)} %copy-done.6) | copy-start | bytes 388
  242.3 4.1 %copy-start.3 = (bf16[1,128,512]{2,1,0:T(8,128)(2,1)S(1)}, bf16[1,128,512]{2,1,0:T(8,128)(2,1)}, u32[]{:S(2)}) copy-start(bf16[1,128,512]{2,1,0:T(8,128)(2,1)} %param.14) | copy-start | bytes 393220
Sparse Core Ops, SparseCore 0:
  66.9 173.7 all-reduce.4
  243.1 122.8 all-reduce.2
Sparse Core Ops, SparseCore 1:
  71.6 93.6 all-gather.1
  246.5 119.7 reduce-scatter.1
where the time goes:
time: 376 us; the launch traced here: 375 us
  waiting for transfers between devices  279 us (74%)
  matrix products  27.4 us (7%)
  starting transfers between devices  23.8 us (6%)
  blocking collectives  19.2 us (5%)
  between operations  16.3 us (4%)
  local copies, waits for them, and re-layouts  4.69 us (1%)
  other arithmetic  4.43 us (1%)
    psum x1, waiting for transfers between devices, body(): total_grads = lax.psum(wide_grads, ('tab', 'dp'))  166 us
    psum x1, waiting for transfers between devices, body(): summed = lax.psum(partial_term, 'col')  112 us
    all_to_all x1, starting transfers between devices, body(): lax.all_to_all(narrow_term.reshape(tab_count, per_device, out_width), 'ta...  23.5 us
    all_gather x1, blocking collectives, body(): piece = lax.all_gather(cotangent, 'col', axis=0, tiled=True)  19.2 us
  transfers between devices with their start and end apart: 5, of which 2 were waited for; matrix products, arithmetic and copies ran while one was open for 7% of the time, Pallas kernels for 0%

commit v1 on v0

v1 whole, which is shorter than its diff:
```python
import functools

import jax
import jax.numpy as jnp
from jax import lax
from jax.experimental import pallas as pl
from jax.experimental.pallas import tpu as pltpu
from jax.sharding import PartitionSpec as P

MESH = pl.DeviceIdType.MESH
BF = jnp.bfloat16
F32 = jnp.float32

NX, NC, NZ, NY, ND = 8, 2, 8, 4, 2
NYF = NY * ND
PER = 32
CH = NY * PER
LONG, SHORT = 4, 3

NT = (((1,), (1,)), ((), ()))
TN = (((0,), (0,)), ((), ()))
NN = (((1,), (0,)), ((), ()))

A_Y = 0
A_Z = A_Y + NY
R_Z = A_Z + 2 * LONG * NY
X_A = R_Z + 2 * LONG
X_S = X_A + NX
W_S = X_S + 1
W_X = W_S + 1
F_Y = W_X + NX
G_Z = F_Y + NY
G_Y = G_Z + NZ
N_X = G_Y + NYF
N_Q = N_X + NX
N_SEM = N_Q + NC * ND


def dot(a, b, dims):
    return lax.dot_general(a, b, dims, preferred_element_type=F32)


def kernel(
    factor,
    wr_h, wl_h, nr_h, nl_h, nw, wp_h, np_h, cot_h,
    o_x, o_wr, o_nr, o_wg, o_ng,
    wr, wl, nr, nl, wp, npj, cot,
    sb, eb, sr, er, wsb, web,
    pooled, mask, wpooled, wterm, ag, cw,
    rs_out, rs_in, wsib, wx_out, wx_in, fz, fy_out, fy_in,
    wg_out, wg_in, wg2_out, wg2_in, ng_acc, ng_out, ng_in, nq_out, nq_in,
    nrg, wrg, xo, wgo, ngo,
    snd, rcv, isem, osem,
):
    col, tab, dp = lax.axis_index("col"), lax.axis_index("tab"), lax.axis_index("dp")
    x, core = col // NC, lax.rem(col, NC)
    z, y = tab // NY, lax.rem(tab, NY)
    yf = y * ND + dp
    sgn = 1 - 2 * core

    def zz(k):
        return lax.rem(z + sgn * k + 4 * NZ, NZ)

    bar = pltpu.get_barrier_semaphore()

    def hello(**dev):
        pl.semaphore_signal(bar, inc=1, device_id=dev, device_id_type=MESH)

    for k in range(1, NYF):
        p = lax.rem(yf + k, NYF)
        hello(tab=z * NY + p // ND, dp=lax.rem(p, ND))
    for k in range(1, NZ):
        hello(tab=lax.rem(z + k, NZ) * NY + y)
    for k in range(1, NX):
        hello(col=lax.rem(x + k, NX) * NC + core)
    hello(col=x * NC + 1 - core)
    hello(col=x * NC + 1 - core, dp=1 - dp)

    loads = [
        pltpu.make_async_copy(s, d, isem.at[i])
        for i, (s, d) in enumerate(
            [(cot_h, cot), (nl_h, nl), (nr_h, nr), (np_h, npj), (wl_h, wl), (wr_h, wr), (wp_h, wp)]
        )
    ]
    for c in loads:
        c.start()
    l_cot, l_nl, l_nr, l_np, l_wl, l_wr, l_wp = loads

    sent = []

    def copy(src, dst, i, **dev):
        return pltpu.make_async_remote_copy(
            src_ref=src, dst_ref=dst, send_sem=snd.at[i], recv_sem=rcv.at[i],
            device_id=dev, device_id_type=MESH,
        )

    def send(*args, **dev):
        c = copy(*args, **dev)
        c.start()
        sent.append(c)
        return c

    l_cot.wait()
    pl.semaphore_wait(bar, (NYF - 1) + (NZ - 1) + (NX - 1) + 2)

    ay = [None]
    for k in range(1, NY):
        p = lax.rem(y + k, NY)
        ay.append(send(cot, ag.at[z, y], A_Y + k, tab=z * NY + p))
    ag[z, y] = cot[...]
    cw[x, core] = cot[...]

    az = {}

    def forward(step, k):
        q = lax.rem(y - k + NY, NY)
        if step < LONG:
            b = zz(-step)
            az[True, step, k] = send(
                ag.at[b, q], ag.at[b, q], A_Z + step * NY + k, tab=zz(1) * NY + y
            )
        if step < SHORT:
            b = zz(step)
            az[False, step, k] = send(
                ag.at[b, q], ag.at[b, q], A_Z + (LONG + step) * NY + k, tab=zz(-1) * NY + y
            )

    def ring(step):
        for k in range(NY):
            if step > 0:
                az[True, step - 1, k].wait_recv()
                if step - 1 < SHORT:
                    az[False, step - 1, k].wait_recv()
            if step < LONG:
                forward(step, k)

    forward(0, 0)
    xa = [None]
    for k in range(1, NX):
        p = lax.rem(x + k, NX)
        xa.append(send(cot, cw.at[x, core], X_A + k, col=p * NC + core))

    l_nl.wait()
    n_narrow = nl.shape[-1]
    lens = jnp.broadcast_to(nl[0].astype(F32), (CH, n_narrow)).astype(BF)
    for c in range(n_narrow // CH):
        row = lax.broadcasted_iota(jnp.int32, (CH, n_narrow), 0) + c * CH
        place = lax.broadcasted_iota(jnp.int32, (CH, n_narrow), 1)
        upto = jnp.where(place <= row, 1.0, 0.0).astype(BF)
        below = jnp.where(place < row, 1.0, 0.0).astype(BF)
        eb[c] = dot(upto, lens, NT).astype(jnp.int32)
        sb[c] = dot(below, lens, NT).astype(jnp.int32)
        er[c] = dot(lens[:16], upto, NT).astype(jnp.int32)
        sr[c] = dot(lens[:16], below, NT).astype(jnp.int32)

    for k in range(1, NY):
        ay[k].wait_recv()
        forward(0, k)

    l_np.wait()
    l_nr.wait()
    n_rows = nr.shape[2]
    slot = nr.shape[3]
    keep = lax.broadcasted_iota(jnp.int32, (2 * CH, slot), 1) < nw[0]
    lane = lax.broadcasted_iota(jnp.int32, (2 * CH, 128), 1)

    def pool(a, b):
        lo = lane - jnp.concatenate([sb[a], sb[b]], axis=0)
        hi = lane - jnp.concatenate([eb[a], eb[b]], axis=0)
        total = jnp.zeros((2 * CH, slot), F32)
        wide = 512
        for r in range(0, n_rows, wide):
            tiles = [
                jnp.where((lo >= -(r + t)) & (hi < -(r + t)), 1.0, 0.0).astype(BF)
                for t in range(0, wide, 128)
            ]
            total += dot(jnp.concatenate(tiles, axis=1), nr[0, 0, r : r + wide, :], NN)
        got = jnp.where(keep, total, 0.0).astype(BF)
        pooled[a] = got[:CH]
        pooled[b] = got[CH:]
        return factor * dot(got, npj[0], NN)

    rs = {}

    def reduce_step(step):
        a, b = zz(LONG - step), zz(step - SHORT)
        term = pool(a, b)
        one, two = term[:CH], term[CH:]
        if step > 0:
            rs[True, step - 1].wait_recv()
            one = one + rs_in[step - 1].astype(F32)
        rs_out[step] = one.astype(BF)
        rs[True, step] = send(rs_out.at[step], rs_in.at[step], R_Z + step, tab=zz(1) * NY + y)
        if step > 0:
            rs[False, step - 1].wait_recv()
            two = two + rs_in[LONG + step - 1].astype(F32)
        if step < SHORT:
            rs_out[LONG + step] = two.astype(BF)
            rs[False, step] = send(
                rs_out.at[LONG + step], rs_in.at[LONG + step], R_Z + LONG + step, tab=zz(-1) * NY + y
            )
        else:
            fz[...] = two

    reduce_step(0)
    ring(1)
    reduce_step(1)

    l_wl.wait()
    n_wide = wl.shape[-1]
    tables = wl.shape[0]
    for w in range(tables):
        wlens = jnp.broadcast_to(wl[w].astype(F32), (128, n_wide)).astype(BF)
        for c in range(n_wide // 128):
            row = lax.broadcasted_iota(jnp.int32, (128, n_wide), 0) + c * 128
            place = lax.broadcasted_iota(jnp.int32, (128, n_wide), 1)
            upto = jnp.where(place <= row, 1.0, 0.0).astype(BF)
            below = jnp.where(place < row, 1.0, 0.0).astype(BF)
            web[w, c] = dot(upto, wlens, NT).astype(jnp.int32)
            wsb[w, c] = dot(below, wlens, NT).astype(jnp.int32)
    ring(2)
    l_wr.wait()
    l_wp.wait()
    w_rows = wr.shape[3]
    w_dim = wr.shape[2]
    wlane = lax.broadcasted_iota(jnp.int32, (128, 128), 1)
    parts = []
    for w in range(tables):
        for c in range(n_wide // 128):
            lo = wlane - wsb[w, c]
            hi = wlane - web[w, c]
            for t in range(0, w_rows, 128):
                mask[w, c * 128 : (c + 1) * 128, t : t + 128] = jnp.where(
                    (lo >= -t) & (hi < -t), 1.0, 0.0
                ).astype(BF)
        parts.append(dot(mask[w], wr[w, 0], NT))
    wpooled[...] = jnp.concatenate(parts, axis=1).astype(BF)
    proj = wp[...].reshape(tables * w_dim, wp.shape[2])
    term = (factor * dot(wpooled[...], proj, NN)).astype(BF)
    wterm[...] = term.reshape(wterm.shape)
    ws = send(wterm.at[:, 1 - core], wsib, W_S, col=x * NC + 1 - core)

    ring(3)
    reduce_step(2)

    ws.wait_recv()
    wx_out[...] = (wterm[:, core].astype(F32) + wsib[...].astype(F32)).astype(BF)
    wx = [None]
    for k in range(1, NX):
        p = lax.rem(x + k, NX)
        wx.append(send(wx_out.at[p], wx_in.at[x], W_X + k, col=p * NC + core))
    wx_in[x] = wx_out[x]

    for k in range(1, NX):
        xa[k].wait_recv()
    xs = send(cw.at[:, core], cw.at[:, core], X_S, col=x * NC + 1 - core)

    ring(4)
    reduce_step(3)

    def back_pair(a, b, first, last):
        both = jnp.concatenate([ag[a].reshape(CH, -1), ag[b].reshape(CH, -1)], axis=0)
        back = jnp.where(keep, factor * dot(both, npj[0], NT), 0.0).astype(BF)
        grads = dot(jnp.concatenate([pooled[a], pooled[b]], axis=0), both, TN)
        if first:
            ng_acc[...] = grads
        elif not last:
            ng_acc[...] += grads
        else:
            grads = (factor * (ng_acc[...] + grads)).T
            ng_out[...] = grads.astype(BF).reshape(ng_out.shape)
            for k in range(1, NX):
                p = lax.rem(x + k, NX)
                nx.append(send(ng_out.at[p], ng_in.at[x], N_X + k, col=p * NC + core))
            ng_in[x] = ng_out[x]
        sub = lax.broadcasted_iota(jnp.int32, (8, 2 * CH), 0)
        lo = sub - jnp.concatenate([sr[a][:8], sr[b][:8]], axis=1)
        hi = sub - jnp.concatenate([er[a][:8], er[b][:8]], axis=1)
        deep = 512
        for r in range(0, n_rows, deep):
            rows = jnp.concatenate(
                [
                    jnp.where((lo >= -(r + g)) & (hi < -(r + g)), 1.0, 0.0)
                    for g in range(0, deep, 8)
                ],
                axis=0,
            ).astype(BF)
            got = dot(rows, back, NN)
            if not first:
                got = got + nrg[r : r + deep, :].astype(F32)
            nrg[r : r + deep, :] = got.astype(BF)
            if last:
                c = pltpu.make_async_copy(
                    nrg.at[r : r + deep], o_nr.at[0, 0, r : r + deep], osem.at[r // deep]
                )
                c.start()
                stores.append(c)

    nx = [None]
    stores = []
    back_pair(zz(-1), zz(1), True, False)
    back_pair(zz(-2), zz(2), False, False)

    xs.wait_recv()
    cols = cw[...].reshape(n_wide, -1)
    wback = (factor * dot(proj, cols, NT)).astype(BF)
    wgrads = (factor * dot(wpooled[...], cols, TN)).T
    wg_out[...] = wgrads.astype(BF).reshape(wg_out.shape)
    gz = [None]
    for k in range(1, NZ):
        p = lax.rem(z + k, NZ)
        gz.append(send(wg_out.at[p], wg_in.at[z], G_Z + k, tab=p * NY + y))
    wg_in[z] = wg_out[z]
    for w in range(tables):
        wrg[w, 0] = dot(wback[w * w_dim : (w + 1) * w_dim], mask[w], NN).astype(BF)
        c = pltpu.make_async_copy(wrg.at[w], o_wr.at[w], osem.at[8 + w])
        c.start()
        stores.append(c)

    rs[True, LONG - 1].wait_recv()
    full = fz[...] + rs_in[LONG - 1].astype(F32)
    fz[...] = full
    fy_out[...] = full.astype(BF).reshape(fy_out.shape)
    fy = [None]
    for k in range(1, NY):
        p = lax.rem(y + k, NY)
        fy.append(send(fy_out.at[p], fy_in.at[y], F_Y + k, tab=z * NY + p))
    fy_in[y] = jnp.zeros(fy_in.shape[1:], BF)

    back_pair(zz(-3), zz(3), False, False)

    for k in range(1, NZ):
        gz[k].wait_recv()
    wsum = jnp.sum(wg_in[...].astype(F32), axis=0)
    wg2_out[...] = wsum.reshape(wg2_out.shape)
    gy = [None]
    for k in range(1, NYF):
        p = lax.rem(yf + k, NYF)
        gy.append(
            send(wg2_out.at[p], wg2_in.at[yf], G_Y + k, tab=z * NY + p // ND, dp=lax.rem(p, ND))
        )
    wg2_in[yf] = wg2_out[yf]

    back_pair(zz(-4), z, False, True)

    for k in range(1, NX):
        nx[k].wait_recv()
    nsum = jnp.sum(ng_in[...].astype(F32), axis=0)
    nq_out[...] = nsum.reshape(nq_out.shape)
    me = core * ND + dp
    nq = [
        send(nq_out.at[(1 - core) * ND + dp], nq_in.at[me], N_Q + 1, col=x * NC + 1 - core),
        send(nq_out.at[core * ND + 1 - dp], nq_in.at[me], N_Q + 2, dp=1 - dp),
        send(
            nq_out.at[(1 - core) * ND + 1 - dp], nq_in.at[me], N_Q + 3,
            col=x * NC + 1 - core, dp=1 - dp,
        ),
    ]
    nq_in[me] = nq_out[me]

    for k in range(1, NY):
        fy[k].wait_recv()
    for k in range(1, NX):
        wx[k].wait_recv()
    total = fz[pl.ds(pl.multiple_of(y * PER, PER), PER), :]
    total = total + jnp.sum(fy_in[...].astype(F32), axis=0) + jnp.sum(wx_in[...].astype(F32), axis=0)
    xo[...] = total.astype(BF)
    c = pltpu.make_async_copy(xo, o_x, osem.at[10])
    c.start()
    stores.append(c)

    for k in range(1, NYF):
        gy[k].wait_recv()
    wout = jnp.sum(wg2_in[...], axis=0)
    for w in range(tables):
        wgo[w] = wout[:, w * w_dim : (w + 1) * w_dim]
    c = pltpu.make_async_copy(wgo, o_wg, osem.at[11])
    c.start()
    stores.append(c)

    for c in nq:
        c.wait_recv()
    ngo[0] = jnp.sum(nq_in[...], axis=0)
    c = pltpu.make_async_copy(ngo, o_ng, osem.at[12])
    c.start()
    stores.append(c)

    for c in sent:
        c.wait_send()
    for c in stores:
        c.wait()


def body(
    wide_rows,
    wide_lengths,
    narrow_rows,
    narrow_lengths,
    narrow_widths,
    wide_proj,
    narrow_proj,
    cotangent,
):
    out_width = cotangent.shape[1]
    tables, _, w_rows, w_dim = wide_rows.shape
    n_rows, slot = narrow_rows.shape[2:]
    n_wide, n_narrow = wide_lengths.shape[2], narrow_lengths.shape[2]
    factor = (tables + narrow_rows.shape[0] * lax.axis_size("tab")) ** (-0.5)
    rows_t = jnp.transpose(wide_rows, (0, 1, 3, 2))
    wk = tables * w_dim
    v = pltpu.VMEM
    scratch = [
        v((tables, 1, w_dim, w_rows), BF), v(wide_lengths.shape, jnp.int32),
        v(narrow_rows.shape, BF), v(narrow_lengths.shape, jnp.int32),
        v(wide_proj.shape, BF), v(narrow_proj.shape, BF), v(cotangent.shape, BF),
        v((NZ, CH, 128), jnp.int32), v((NZ, CH, 128), jnp.int32),
        v((NZ, 16, 128), jnp.int32), v((NZ, 16, 128), jnp.int32),
        v((tables, n_wide // 128, 128, 128), jnp.int32), v((tables, n_wide // 128, 128, 128), jnp.int32),
        v((NZ, CH, slot), BF), v((tables, n_wide, w_rows), BF), v((n_wide, wk), BF),
        v((NX, NC, PER, out_width), BF), v((NZ, NY, PER, out_width), BF), v((NX, NC, PER, out_width), BF),
        v((LONG + SHORT, CH, out_width), BF), v((LONG + SHORT, CH, out_width), BF),
        v((NX, PER, out_width), BF), v((NX, PER, out_width), BF), v((NX, PER, out_width), BF),
        v((CH, out_width), F32), v((NY, PER, out_width), BF), v((NY, PER, out_width), BF),
        v((NZ, out_width // NZ, wk), BF), v((NZ, out_width // NZ, wk), BF),
        v((NYF, out_width // NZ // NYF, wk), F32), v((NYF, out_width // NZ // NYF, wk), F32),
        v((slot, out_width), F32), v((NX, out_width // NX, slot), BF), v((NX, out_width // NX, slot), BF),
        v((NC * ND, out_width // NX // NC // ND, slot), F32), v((NC * ND, out_width // NX // NC // ND, slot), F32),
        v((n_rows, slot), BF), v((tables, 1, w_dim, w_rows), BF), v((PER, out_width), BF),
        v((tables, out_width // NZ // NYF, w_dim), F32), v((1, out_width // NX // NC // ND, slot), F32),
        pltpu.SemaphoreType.DMA((N_SEM,)), pltpu.SemaphoreType.DMA((N_SEM,)),
        pltpu.SemaphoreType.DMA((8,)), pltpu.SemaphoreType.DMA((16,)),
    ]
    hbm = pl.BlockSpec(memory_space=pl.ANY)
    smem = pl.BlockSpec(memory_space=pltpu.SMEM)
    s = jax.ShapeDtypeStruct
    outs = pl.pallas_call(
        functools.partial(kernel, factor),
        name="sparse_arch",
        out_shape=(
            s((PER, out_width), BF),
            s((tables, 1, w_dim, w_rows), BF),
            s(narrow_rows.shape, BF),
            s((tables, out_width // NZ // NYF, w_dim), F32),
            s((1, out_width // NX // NC // ND, slot), F32),
        ),
        in_specs=[hbm, hbm, hbm, hbm, smem, hbm, hbm, hbm],
        out_specs=(hbm,) * 5,
        scratch_shapes=scratch,
        compiler_params=pltpu.CompilerParams(
            collective_id=0, has_side_effects=True, vmem_limit_bytes=48 * 1024 * 1024
        ),
    )(rows_t, wide_lengths, narrow_rows, narrow_lengths, narrow_widths, wide_proj, narrow_proj, cotangent)
    cross, wide_t, narrow, wide_g, narrow_g = outs
    return (
        cross,
        jnp.transpose(wide_t, (0, 1, 3, 2)),
        narrow,
        jnp.transpose(wide_g, (0, 2, 1)),
        jnp.transpose(narrow_g, (0, 2, 1)),
    )


def solution(mesh):
    in_specs = (
        P(None, ("tab", "dp"), None, "col"),
        P(None, ("tab", "dp"), None),
        P("tab", ("col", "dp"), None, None),
        P("tab", ("col", "dp"), None),
        P("tab"),
        P(None, "col", None),
        P("tab", None, None),
        P(("col", "tab", "dp"), None),
    )
    out_specs = (
        P(("col", "tab", "dp"), None),
        P(None, ("tab", "dp"), None, "col"),
        P("tab", ("col", "dp"), None, None),
        P(None, "col", ("tab", "dp")),
        P("tab", None, ("col", "dp")),
    )
    return jax.shard_map(body, mesh=mesh, in_specs=in_specs, out_specs=out_specs, check_vma=False)
```

time: 376 us -> 79.6 us (0.21)
  waiting for transfers between devices: 279 us -> 0 us
  Pallas kernels: 0 us -> 68.1 us
  matrix products: 27.4 us -> 0 us
  starting transfers between devices: 23.8 us -> 0 us
  blocking collectives: 19.2 us -> 0 us
  between operations: 16.3 us -> 1.3 us
  local copies, waits for them, and re-layouts: 4.69 us -> 9.77 us
  other arithmetic: 4.43 us -> 0 us
    psum x2 -> x0, waiting for transfers between devices: 279 us -> none  [the longest x1 166 us: body(): total_grads = lax.psum(wide_grads, ('tab', 'dp'))]
    pallas_call x0 -> x1, Pallas kernels: none -> 68.1 us  [body(): pl.pallas_call(functools.partial(kernel, factor), name='sparse_arch', out...]
    dot_general x8 -> x0, matrix products: 27.4 us -> none  [the longest x1 7.1 us: body(): jnp.einsum('tsr,tsk->trk', narrow_masks, narrow_backs, preferred_element_...]
    all_to_all x1 -> x0, starting transfers between devices: 23.5 us -> none  [body(): lax.all_to_all(narrow_term.reshape(tab_count, per_device, out_width), 'ta...]
    all_gather x1 -> x0, blocking collectives: 19.2 us -> none  [body(): piece = lax.all_gather(cotangent, 'col', axis=0, tiled=True)]
    unnamed x18 -> x19, local copies, waits for them, and re-layouts: 1.51 us -> 9.77 us
  transfers between devices with their start and end apart: 5 -> 0, of which waited for: 2 -> 0; matrix products, arithmetic and copies ran while one was open for 7% -> 0% of each run, Pallas kernels for 0% -> 0%
where the time goes in v1:
time: 79.6 us; the launch traced here: 79.2 us
  Pallas kernels  68.1 us (86%)
  local copies, waits for them, and re-layouts  9.77 us (12%)
  between operations  1.3 us (2%)
    pallas_call x1, Pallas kernels, body(): pl.pallas_call(functools.partial(kernel, factor), name='sparse_arch', out...  68.1 us
    unnamed x19, local copies, waits for them, and re-layouts  9.77 us

profile of v1, /device:TPU:1, one launch (start us, length us, event | category | flops | bytes accessed | tf_op | source)
XLA Modules:
  0.0 79.2 jit_solution(6849020383590438393)
XLA Ops:
  1.3 0.0 copy-start
  1.3 1.2 %copy-done = bf16[1,1,4096,128]{3,2,1,0:T(8,128)(2,1)S(1)} copy-done((bf16[1,1,4096,128]{3,2,1,0:T(8,128)(2,1)S(1)}, bf16[1,1,4096,128]{3,2,1,0:T(8,128)(2,1)}, u32[]{:S(2)}) %copy-start) | copy-done | bytes 1048600
  2.5 0.0 copy-start.1
  2.5 1.0 %copy-done.1 = bf16[2,1,2048,64]{2,3,1,0:T(8,128)(2,1)S(1)} copy-done((bf16[2,1,2048,64]{2,3,1,0:T(8,128)(2,1)S(1)}, bf16[2,1,2048,64]{2,3,1,0:T(8,128)(2,1)}, u32[]{:S(2)}) %copy-start.1) | copy-done | bytes 524312
  3.5 0.0 copy-start.2
  3.5 0.9 %copy-done.2 = bf16[2,64,512]{2,1,0:T(8,128)(2,1)S(1)} copy-done((bf16[2,64,512]{2,1,0:T(8,128)(2,1)S(1)}, bf16[2,64,512]{2,1,0:T(8,128)(2,1)}, u32[]{:S(2)}) %copy-start.2) | copy-done | bytes 131096
  4.5 0.0 copy-start.3
  4.5 0.9 %copy-done.3 = bf16[1,128,512]{2,1,0:T(8,128)(2,1)S(1)} copy-done((bf16[1,128,512]{2,1,0:T(8,128)(2,1)S(1)}, bf16[1,128,512]{2,1,0:T(8,128)(2,1)}, u32[]{:S(2)}) %copy-start.3) | copy-done | bytes 131096
  5.4 0.0 copy-start.4
  5.4 0.8 copy-done.4
  6.1 0.0 copy-start.5
  6.1 0.7 copy-done.5
  6.8 0.0 copy-start.6
  6.8 0.7 copy-done.6
  7.5 68.1 %sparse_arch.1 = (bf16[32,512]{1,0:T(8,128)(2,1)S(1)}, bf16[2,1,64,2048]{3,2,1,0:T(8,128)(2,1)S(1)}, bf16[1,1,4096,128]{3,2,1,0:T(8,128)(2,1)S(1)}, f32[2,8,64]{2,1,0:T(8,128)S(1)}, f32[1,16,128]{2,1,0:T(8,128)S(1)}) custom-call(bf16[2,1,64,2048]{3,2,1,0:T(8,128)(2,1)S(1)} %bitcast.5, s32[2,1,512]{2,1,0:T(1,128)S(1)} %copy-done.5, ...), custom_call_target="tpu_custom_call" | custom-call | tf_op jit(solution)/shard_map/sparse_arch/pallas_call | solution.py:436
  75.6 0.6 copy.19
  76.2 0.8 %copy.20 = bf16[2,1,2048,64]{2,3,1,0:T(8,128)(2,1)} copy(bf16[2,1,2048,64]{2,3,1,0:T(8,128)(2,1)S(1)} %bitcast.4) | data formatting | bytes 1048576
  77.0 1.0 %copy.21 = bf16[1,1,4096,128]{3,2,1,0:T(8,128)(2,1)} copy(bf16[1,1,4096,128]{3,2,1,0:T(8,128)(2,1)S(1)} %get-tuple-element.22) | data formatting | bytes 2097152
  78.0 0.6 copy.22
  78.6 0.6 copy.23
Async XLA Ops:
  1.3 1.2 %copy-start = (bf16[1,1,4096,128]{3,2,1,0:T(8,128)(2,1)S(1)}, bf16[1,1,4096,128]{3,2,1,0:T(8,128)(2,1)}, u32[]{:S(2)}) copy-start(bf16[1,1,4096,128]{3,2,1,0:T(8,128)(2,1)} %nr_h.1) | copy-start | bytes 3145732
  2.5 1.0 %copy-start.1 = (bf16[2,1,2048,64]{2,3,1,0:T(8,128)(2,1)S(1)}, bf16[2,1,2048,64]{2,3,1,0:T(8,128)(2,1)}, u32[]{:S(2)}) copy-start(bf16[2,1,2048,64]{2,3,1,0:T(8,128)(2,1)} %param.8) | copy-start | bytes 1572868
  3.5 0.9 %copy-start.2 = (bf16[2,64,512]{2,1,0:T(8,128)(2,1)S(1)}, bf16[2,64,512]{2,1,0:T(8,128)(2,1)}, u32[]{:S(2)}) copy-start(bf16[2,64,512]{2,1,0:T(8,128)(2,1)} %wp_h.1) | copy-start | bytes 393220
  4.5 0.9 %copy-start.3 = (bf16[1,128,512]{2,1,0:T(8,128)(2,1)S(1)}, bf16[1,128,512]{2,1,0:T(8,128)(2,1)}, u32[]{:S(2)}) copy-start(bf16[1,128,512]{2,1,0:T(8,128)(2,1)} %np_h.1) | copy-start | bytes 393220
  5.4 0.8 copy-start.4
  6.1 0.7 copy-start.5
  6.8 0.7 copy-start.6

commit v2 on v1

--- a/solution.py
+++ b/solution.py
@@ -13,6 +13,7 @@
 
 NX, NC, NZ, NY, ND = 8, 2, 8, 4, 2
 NYF = NY * ND
+VMEM = 56 * 1024 * 1024
 PER = 32
 CH = NY * PER
 LONG, SHORT = 4, 3
@@ -24,13 +25,13 @@
 A_Y = 0
 A_Z = A_Y + NY
 R_Z = A_Z + 2 * LONG * NY
-X_A = R_Z + 2 * LONG
+X_A = R_Z + 2 * LONG * NY
 X_S = X_A + NX
 W_S = X_S + 1
 W_X = W_S + 1
 F_Y = W_X + NX
-G_Z = F_Y + NY
-G_Y = G_Z + NZ
+G_Z = F_Y + NY * NY
+G_Y = G_Z + LONG + SHORT
 N_X = G_Y + NYF
 N_Q = N_X + NX
 N_SEM = N_Q + NC * ND
@@ -48,8 +49,8 @@
     sb, eb, sr, er, wsb, web,
     pooled, mask, wpooled, wterm, ag, cw,
     rs_out, rs_in, wsib, wx_out, wx_in, fz, fy_out, fy_in,
-    wg_out, wg_in, wg2_out, wg2_in, ng_acc, ng_out, ng_in, nq_out, nq_in,
-    nrg, wrg, xo, wgo, ngo,
+    wg, wgz, wg_out, wg_in, wg2_out, wg2_in, ng_acc, ng_out, ng_in, nq_out, nq_in,
+    back, nrg, wrg, xo, wgo, ngo,
     snd, rcv, isem, osem,
 ):
     col, tab, dp = lax.axis_index("col"), lax.axis_index("tab"), lax.axis_index("dp")
@@ -69,7 +70,7 @@
     for k in range(1, NYF):
         p = lax.rem(yf + k, NYF)
         hello(tab=z * NY + p // ND, dp=lax.rem(p, ND))
-    for k in range(1, NZ):
+    for k in (1, NZ - 1):
         hello(tab=lax.rem(z + k, NZ) * NY + y)
     for k in range(1, NX):
         hello(col=lax.rem(x + k, NX) * NC + core)
@@ -86,7 +87,13 @@
         c.start()
     l_cot, l_nl, l_nr, l_np, l_wl, l_wr, l_wp = loads
 
-    sent = []
+    sent, stores = [], []
+
+    def keep_out(src, dst):
+        c = pltpu.make_async_copy(src, dst, osem.at[len(stores)])
+        c.start()
+        stores.append(c)
+
 
     def copy(src, dst, i, **dev):
         return pltpu.make_async_remote_copy(
@@ -101,7 +108,7 @@
         return c
 
     l_cot.wait()
-    pl.semaphore_wait(bar, (NYF - 1) + (NZ - 1) + (NX - 1) + 2)
+    pl.semaphore_wait(bar, (NYF - 1) + 2 + (NX - 1) + 2)
 
     ay = [None]
     for k in range(1, NY):
@@ -125,14 +132,12 @@
                 ag.at[b, q], ag.at[b, q], A_Z + (LONG + step) * NY + k, tab=zz(-1) * NY + y
             )
 
-    def ring(step):
-        for k in range(NY):
-            if step > 0:
-                az[True, step - 1, k].wait_recv()
-                if step - 1 < SHORT:
-                    az[False, step - 1, k].wait_recv()
-            if step < LONG:
-                forward(step, k)
+    def ring(step, k):
+        az[True, step - 1, k].wait_recv()
+        if step - 1 < SHORT:
+            az[False, step - 1, k].wait_recv()
+        if step < LONG:
+            forward(step, k)
 
     forward(0, 0)
     xa = [None]
@@ -182,29 +187,42 @@
 
     rs = {}
 
-    def reduce_step(step):
-        a, b = zz(LONG - step), zz(step - SHORT)
-        term = pool(a, b)
-        one, two = term[:CH], term[CH:]
+    def reduce_long(step, q, mine):
         if step > 0:
-            rs[True, step - 1].wait_recv()
-            one = one + rs_in[step - 1].astype(F32)
-        rs_out[step] = one.astype(BF)
-        rs[True, step] = send(rs_out.at[step], rs_in.at[step], R_Z + step, tab=zz(1) * NY + y)
+            rs[True, step - 1, q].wait_recv()
+            mine = mine + rs_in[step - 1, q].astype(F32)
+        rs_out[step, q] = mine.astype(BF)
+        rs[True, step, q] = send(
+            rs_out.at[step, q], rs_in.at[step, q], R_Z + step * NY + q, tab=zz(1) * NY + y
+        )
+
+    def reduce_short(step, q, mine):
         if step > 0:
-            rs[False, step - 1].wait_recv()
-            two = two + rs_in[LONG + step - 1].astype(F32)
+            rs[False, step - 1, q].wait_recv()
+            mine = mine + rs_in[LONG + step - 1, q].astype(F32)
         if step < SHORT:
-            rs_out[LONG + step] = two.astype(BF)
-            rs[False, step] = send(
-                rs_out.at[LONG + step], rs_in.at[LONG + step], R_Z + LONG + step, tab=zz(-1) * NY + y
+            rs_out[LONG + step, q] = mine.astype(BF)
+            rs[False, step, q] = send(
+                rs_out.at[LONG + step, q], rs_in.at[LONG + step, q],
+                R_Z + (LONG + step) * NY + q, tab=zz(-1) * NY + y,
             )
         else:
-            fz[...] = two
-
-    reduce_step(0)
-    ring(1)
-    reduce_step(1)
+            fz[q] = mine
+
+    def reduce_step(step, term):
+        for q in range(NY):
+            reduce_long(step, q, term[q * PER : (q + 1) * PER])
+            reduce_short(step, q, term[CH + q * PER : CH + (q + 1) * PER])
+
+    def gather_step(step):
+        for k in range(NY):
+            ring(step, k)
+
+    term = pool(zz(LONG), zz(-SHORT))
+    reduce_step(0, term)
+    term = pool(zz(LONG - 1), zz(1 - SHORT))
+    gather_step(1)
+    reduce_step(1, term)
 
     l_wl.wait()
     n_wide = wl.shape[-1]
@@ -218,7 +236,6 @@
             below = jnp.where(place < row, 1.0, 0.0).astype(BF)
             web[w, c] = dot(upto, wlens, NT).astype(jnp.int32)
             wsb[w, c] = dot(below, wlens, NT).astype(jnp.int32)
-    ring(2)
     l_wr.wait()
     l_wp.wait()
     w_rows = wr.shape[3]
@@ -239,40 +256,20 @@
     term = (factor * dot(wpooled[...], proj, NN)).astype(BF)
     wterm[...] = term.reshape(wterm.shape)
     ws = send(wterm.at[:, 1 - core], wsib, W_S, col=x * NC + 1 - core)
-
-    ring(3)
-    reduce_step(2)
-
-    ws.wait_recv()
-    wx_out[...] = (wterm[:, core].astype(F32) + wsib[...].astype(F32)).astype(BF)
-    wx = [None]
-    for k in range(1, NX):
-        p = lax.rem(x + k, NX)
-        wx.append(send(wx_out.at[p], wx_in.at[x], W_X + k, col=p * NC + core))
-    wx_in[x] = wx_out[x]
-
     for k in range(1, NX):
         xa[k].wait_recv()
     xs = send(cw.at[:, core], cw.at[:, core], X_S, col=x * NC + 1 - core)
 
-    ring(4)
-    reduce_step(3)
-
-    def back_pair(a, b, first, last):
+    def grads_pair(a, b, i):
         both = jnp.concatenate([ag[a].reshape(CH, -1), ag[b].reshape(CH, -1)], axis=0)
-        back = jnp.where(keep, factor * dot(both, npj[0], NT), 0.0).astype(BF)
+        back[i] = jnp.where(keep, factor * dot(both, npj[0], NT), 0.0).astype(BF)
         grads = dot(jnp.concatenate([pooled[a], pooled[b]], axis=0), both, TN)
-        if first:
+        if i == 0:
             ng_acc[...] = grads
-        elif not last:
+        else:
             ng_acc[...] += grads
-        else:
-            grads = (factor * (ng_acc[...] + grads)).T
-            ng_out[...] = grads.astype(BF).reshape(ng_out.shape)
-            for k in range(1, NX):
-                p = lax.rem(x + k, NX)
-                nx.append(send(ng_out.at[p], ng_in.at[x], N_X + k, col=p * NC + core))
-            ng_in[x] = ng_out[x]
+
+    def rows_pair(a, b, i):
         sub = lax.broadcasted_iota(jnp.int32, (8, 2 * CH), 0)
         lo = sub - jnp.concatenate([sr[a][:8], sr[b][:8]], axis=1)
         hi = sub - jnp.concatenate([er[a][:8], er[b][:8]], axis=1)
@@ -285,63 +282,84 @@
                 ],
                 axis=0,
             ).astype(BF)
-            got = dot(rows, back, NN)
-            if not first:
+            got = dot(rows, back[i], NN)
+            if i > 0:
                 got = got + nrg[r : r + deep, :].astype(F32)
             nrg[r : r + deep, :] = got.astype(BF)
-            if last:
-                c = pltpu.make_async_copy(
-                    nrg.at[r : r + deep], o_nr.at[0, 0, r : r + deep], osem.at[r // deep]
-                )
-                c.start()
-                stores.append(c)
-
-    nx = [None]
-    stores = []
-    back_pair(zz(-1), zz(1), True, False)
-    back_pair(zz(-2), zz(2), False, False)
+            if i == LONG - 1:
+                keep_out(nrg.at[r : r + deep], o_nr.at[0, 0, r : r + deep])
+
+    gr = {}
+
+    def wide_step(step):
+        one, two = wg[zz(LONG - step)], wg[zz(step - SHORT)]
+        if step > 0:
+            gr[True, step - 1].wait_recv()
+            one = one + wg_in[step - 1].astype(F32)
+            gr[False, step - 1].wait_recv()
+            two = two + wg_in[LONG + step - 1].astype(F32)
+        wg_out[step] = one.astype(BF)
+        gr[True, step] = send(wg_out.at[step], wg_in.at[step], G_Z + step, tab=zz(1) * NY + y)
+        if step < SHORT:
+            wg_out[LONG + step] = two.astype(BF)
+            gr[False, step] = send(
+                wg_out.at[LONG + step], wg_in.at[LONG + step], G_Z + LONG + step, tab=zz(-1) * NY + y
+            )
+        else:
+            wgz[...] = two
+
+    term = pool(zz(LONG - 2), zz(2 - SHORT))
+    gather_step(2)
+    reduce_step(2, term)
+
+    ws.wait_recv()
+    wx_out[...] = (wterm[:, core].astype(F32) + wsib[...].astype(F32)).astype(BF)
+    wx = [None]
+    for k in range(1, NX):
+        p = lax.rem(x + k, NX)
+        wx.append(send(wx_out.at[p], wx_in.at[x], W_X + k, col=p * NC + core))
+    wx_in[x] = wx_out[x]
 
     xs.wait_recv()
     cols = cw[...].reshape(n_wide, -1)
-    wback = (factor * dot(proj, cols, NT)).astype(BF)
-    wgrads = (factor * dot(wpooled[...], cols, TN)).T
-    wg_out[...] = wgrads.astype(BF).reshape(wg_out.shape)
-    gz = [None]
-    for k in range(1, NZ):
-        p = lax.rem(z + k, NZ)
-        gz.append(send(wg_out.at[p], wg_in.at[z], G_Z + k, tab=p * NY + y))
-    wg_in[z] = wg_out[z]
-    for w in range(tables):
-        wrg[w, 0] = dot(wback[w * w_dim : (w + 1) * w_dim], mask[w], NN).astype(BF)
-        c = pltpu.make_async_copy(wrg.at[w], o_wr.at[w], osem.at[8 + w])
-        c.start()
-        stores.append(c)
-
-    rs[True, LONG - 1].wait_recv()
-    full = fz[...] + rs_in[LONG - 1].astype(F32)
-    fz[...] = full
-    fy_out[...] = full.astype(BF).reshape(fy_out.shape)
-    fy = [None]
-    for k in range(1, NY):
-        p = lax.rem(y + k, NY)
-        fy.append(send(fy_out.at[p], fy_in.at[y], F_Y + k, tab=z * NY + p))
+    wg[...] = (factor * dot(wpooled[...], cols, TN)).T.reshape(wg.shape)
+    wide_step(0)
+
+    term = pool(zz(LONG - 3), z)
+    grads_pair(zz(-1), zz(1), 0)
+    rows_pair(zz(-1), zz(1), 0)
+    gather_step(3)
+    reduce_step(3, term)
+    wide_step(1)
+
+    grads_pair(zz(-2), zz(2), 1)
+    grads_pair(zz(-3), zz(3), 2)
+    rows_pair(zz(-2), zz(2), 1)
+
+    gather_step(LONG)
+    grads_pair(zz(-4), z, 3)
+    ng_out[...] = (factor * ng_acc[...]).T.astype(BF).reshape(ng_out.shape)
+    nx = [None]
+    for k in range(1, NX):
+        p = lax.rem(x + k, NX)
+        nx.append(send(ng_out.at[p], ng_in.at[x], N_X + k, col=p * NC + core))
+    ng_in[x] = ng_out[x]
+    wide_step(2)
+
+    rows_pair(zz(-3), zz(3), 2)
+
+    for q in range(NY):
+        rs[True, LONG - 1, q].wait_recv()
+        full = fz[q] + rs_in[LONG - 1, q].astype(F32)
+        fz[q] = full
+        fy_out[q] = full.astype(BF)
+
+        @pl.when(y != q)
+        def _():
+            copy(fy_out.at[q], fy_in.at[y], F_Y + q * NY + y, tab=z * NY + q).start()
+
     fy_in[y] = jnp.zeros(fy_in.shape[1:], BF)
-
-    back_pair(zz(-3), zz(3), False, False)
-
-    for k in range(1, NZ):
-        gz[k].wait_recv()
-    wsum = jnp.sum(wg_in[...].astype(F32), axis=0)
-    wg2_out[...] = wsum.reshape(wg2_out.shape)
-    gy = [None]
-    for k in range(1, NYF):
-        p = lax.rem(yf + k, NYF)
-        gy.append(
-            send(wg2_out.at[p], wg2_in.at[yf], G_Y + k, tab=z * NY + p // ND, dp=lax.rem(p, ND))
-        )
-    wg2_in[yf] = wg2_out[yf]
-
-    back_pair(zz(-4), z, False, True)
+    wide_step(3)
 
     for k in range(1, NX):
         nx[k].wait_recv()
@@ -358,37 +376,65 @@
     ]
     nq_in[me] = nq_out[me]
 
+    wback = (factor * dot(proj, cw[...].reshape(n_wide, -1), NT)).astype(BF)
+    for w in range(tables):
+        wrg[w, 0] = dot(wback[w * w_dim : (w + 1) * w_dim], mask[w], NN).astype(BF)
+        keep_out(wrg.at[w], o_wr.at[w])
+
+    gr[True, LONG - 1].wait_recv()
+    wsum = wgz[...] + wg_in[LONG - 1].astype(F32)
+    wg2_out[...] = wsum.reshape(wg2_out.shape)
+    gy = [None]
+    for k in range(1, NYF):
+        p = lax.rem(yf + k, NYF)
+        gy.append(
+            send(wg2_out.at[p], wg2_in.at[yf], G_Y + k, tab=z * NY + p // ND, dp=lax.rem(p, ND))
+        )
+    wg2_in[yf] = wg2_out[yf]
+
+    rows_pair(zz(-4), z, 3)
+
     for k in range(1, NY):
-        fy[k].wait_recv()
+        p = lax.rem(y + k, NY)
+        copy(fy_out.at[p], fy_in.at[p], F_Y + y * NY + p, tab=z * NY + p).wait_recv()
+        copy(fy_out.at[p], fy_in.at[y], F_Y + p * NY + y, tab=z * NY + p).wait_send()
     for k in range(1, NX):
         wx[k].wait_recv()
-    total = fz[pl.ds(pl.multiple_of(y * PER, PER), PER), :]
-    total = total + jnp.sum(fy_in[...].astype(F32), axis=0) + jnp.sum(wx_in[...].astype(F32), axis=0)
+    total = fz[y] + jnp.sum(fy_in[...].astype(F32), axis=0) + jnp.sum(wx_in[...].astype(F32), axis=0)
     xo[...] = total.astype(BF)
-    c = pltpu.make_async_copy(xo, o_x, osem.at[10])
-    c.start()
-    stores.append(c)
+    keep_out(xo, o_x)
 
     for k in range(1, NYF):
         gy[k].wait_recv()
     wout = jnp.sum(wg2_in[...], axis=0)
     for w in range(tables):
         wgo[w] = wout[:, w * w_dim : (w + 1) * w_dim]
-    c = pltpu.make_async_copy(wgo, o_wg, osem.at[11])
-    c.start()
-    stores.append(c)
+    keep_out(wgo, o_wg)
 
     for c in nq:
         c.wait_recv()
     ngo[0] = jnp.sum(nq_in[...], axis=0)
-    c = pltpu.make_async_copy(ngo, o_ng, osem.at[12])
-    c.start()
-    stores.append(c)
+    keep_out(ngo, o_ng)
 
     for c in sent:
         c.wait_send()
     for c in stores:
         c.wait()
+
+
+def store(*refs):
+    n = len(refs) // 3
+    src, dst, held, sem = refs[:n], refs[n : 2 * n], refs[2 * n : 3 * n], refs[3 * n]
+    order = sorted(range(n), key=lambda i: -src[i].size)
+    come = {i: pltpu.make_async_copy(src[i], held[i], sem.at[i]) for i in order}
+    go = {i: pltpu.make_async_copy(held[i], dst[i], sem.at[n + i]) for i in order}
+    for i in order:
+        come[i].start()
+    for i in reversed(order):
+        come[i].wait()
+        go[i].start()
+    for i in order:
+        go[i].wait()
 
 
 def body(
@@ -418,14 +464,15 @@
         v((tables, n_wide // 128, 128, 128), jnp.int32), v((tables, n_wide // 128, 128, 128), jnp.int32),
         v((NZ, CH, slot), BF), v((tables, n_wide, w_rows), BF), v((n_wide, wk), BF),
         v((NX, NC, PER, out_width), BF), v((NZ, NY, PER, out_width), BF), v((NX, NC, PER, out_width), BF),
-        v((LONG + SHORT, CH, out_width), BF), v((LONG + SHORT, CH, out_width), BF),
+        v((LONG + SHORT, NY, PER, out_width), BF), v((LONG + SHORT, NY, PER, out_width), BF),
         v((NX, PER, out_width), BF), v((NX, PER, out_width), BF), v((NX, PER, out_width), BF),
-        v((CH, out_width), F32), v((NY, PER, out_width), BF), v((NY, PER, out_width), BF),
-        v((NZ, out_width // NZ, wk), BF), v((NZ, out_width // NZ, wk), BF),
+        v((NY, PER, out_width), F32), v((NY, PER, out_width), BF), v((NY, PER, out_width), BF),
+        v((NZ, out_width // NZ, wk), F32), v((out_width // NZ, wk), F32),
+        v((LONG + SHORT, out_width // NZ, wk), BF), v((LONG + SHORT, out_width // NZ, wk), BF),
         v((NYF, out_width // NZ // NYF, wk), F32), v((NYF, out_width // NZ // NYF, wk), F32),
         v((slot, out_width), F32), v((NX, out_width // NX, slot), BF), v((NX, out_width // NX, slot), BF),
         v((NC * ND, out_width // NX // NC // ND, slot), F32), v((NC * ND, out_width // NX // NC // ND, slot), F32),
-        v((n_rows, slot), BF), v((tables, 1, w_dim, w_rows), BF), v((PER, out_width), BF),
+        v((LONG, 2 * CH, slot), BF), v((n_rows, slot), BF), v((tables, 1, w_dim, w_rows), BF), v((PER, out_width), BF),
         v((tables, out_width // NZ // NYF, w_dim), F32), v((1, out_width // NX // NC // ND, slot), F32),
         pltpu.SemaphoreType.DMA((N_SEM,)), pltpu.SemaphoreType.DMA((N_SEM,)),
         pltpu.SemaphoreType.DMA((8,)), pltpu.SemaphoreType.DMA((16,)),
@@ -447,10 +494,18 @@
         out_specs=(hbm,) * 5,
         scratch_shapes=scratch,
         compiler_params=pltpu.CompilerParams(
-            collective_id=0, has_side_effects=True, vmem_limit_bytes=48 * 1024 * 1024
+            collective_id=0, has_side_effects=True, vmem_limit_bytes=VMEM
         ),
     )(rows_t, wide_lengths, narrow_rows, narrow_lengths, narrow_widths, wide_proj, narrow_proj, cotangent)
-    cross, wide_t, narrow, wide_g, narrow_g = outs
+    cross, wide_t, narrow, wide_g, narrow_g = pl.pallas_call(
+        store,
+        name="store",
+        out_shape=[s(o.shape, o.dtype) for o in outs],
+        in_specs=[hbm] * len(outs),
+        out_specs=[hbm] * len(outs),
+        scratch_shapes=[v(o.shape, o.dtype) for o in outs] + [pltpu.SemaphoreType.DMA((2 * len(outs),))],
+        compiler_params=pltpu.CompilerParams(vmem_limit_bytes=VMEM),
+    )(*outs)
     return (
         cross,
         jnp.transpose(wide_t, (0, 1, 3, 2)),

time: 79.6 us -> 67.8 us (0.85)
  the two profiles are of different devices: /device:TPU:1 before, /device:TPU:16 now
where the time goes in v2:
time: 67.8 us; the launch traced here: 67.6 us
  Pallas kernels  66.3 us (98%)
  between operations  1.29 us (2%)
    pallas_call x1, Pallas kernels, body(): pl.pallas_call(functools.partial(kernel, factor), name='sparse_arch', out...  63.8 us
    pallas_call x1, Pallas kernels, body(): pl.pallas_call(store, name='store', out_shape=[s(o.shape, o.dtype) for o...  2.6 us

profile of v2, /device:TPU:16, one launch (start us, length us, event | category | flops | bytes accessed | tf_op | source)
XLA Modules:
  0.0 67.6 jit_solution(12151386747090497184)
XLA Ops:
  1.3 63.8 %sparse_arch.1 = (bf16[32,512]{1,0:T(8,128)(2,1)}, bf16[2,1,64,2048]{3,2,1,0:T(8,128)(2,1)}, bf16[1,1,4096,128]{3,2,1,0:T(8,128)(2,1)}, f32[2,8,64]{2,1,0:T(8,128)}, f32[1,16,128]{2,1,0:T(8,128)}) custom-call(bf16[2,1,64,2048]{3,2,1,0:T(8,128)(2,1)} %bitcast.4, s32[2,1,512]{2,1,0:T(1,128)} %wl_h.1, bf16[1,1,4096,128]{3,2,1,0:T(8,128)(2,1)} %nr_h.1, ...), custom_call_target="tpu_custom_call" | custom-call | tf_op jit(solution)/shard_map/sparse_arch/pallas_call | solution.py:483
  65.0 2.6 %store.1 = (bf16[32,512]{1,0:T(8,128)(2,1)}, bf16[2,1,64,2048]{3,2,1,0:T(8,128)(2,1)}, bf16[1,1,4096,128]{3,2,1,0:T(8,128)(2,1)}, f32[2,8,64]{2,1,0:T(8,128)}, f32[1,16,128]{2,1,0:T(8,128)}) custom-call(bf16[32,512]{1,0:T(8,128)(2,1)} %get-tuple-element.15.refs_0_, bf16[2,1,64,2048]{3,2,1,0:T(8,128)(2,1)} %get-tuple-element.16.refs_1_, ...), custom_call_target="tpu_custom_call" | custom-call | tf_op jit(solution)/shard_map/store/pallas_call | solution.py:500

commit v3 on v2

--- a/solution.py
+++ b/solution.py
@@ -13,6 +13,7 @@
 
 NX, NC, NZ, NY, ND = 8, 2, 8, 4, 2
 NYF = NY * ND
+STORE_PARTS = 4
 VMEM = 56 * 1024 * 1024
 PER = 32
 CH = NY * PER
@@ -422,19 +423,29 @@
         c.wait()
 
 
+def pieces(shape):
+    if len(shape) < 4:
+        return [()]
+    rows = shape[2] // STORE_PARTS
+    return [(w, 0, pl.ds(i * rows, rows)) for w in range(shape[0]) for i in range(STORE_PARTS)]
+
+
 def store(*refs):
     n = len(refs) // 3
     src, dst, held, sem = refs[:n], refs[n : 2 * n], refs[2 * n : 3 * n], refs[3 * n]
-    order = sorted(range(n), key=lambda i: -src[i].size)
-    come = {i: pltpu.make_async_copy(src[i], held[i], sem.at[i]) for i in order}
-    go = {i: pltpu.make_async_copy(held[i], dst[i], sem.at[n + i]) for i in order}
-    for i in order:
-        come[i].start()
-    for i in reversed(order):
-        come[i].wait()
-        go[i].start()
-    for i in order:
-        go[i].wait()
+    parts = [(i, at) for i in range(n) for at in pieces(src[i].shape)]
+    come, go = [], []
+    for j, (i, at) in enumerate(parts):
+        s, h, d = (r.at[at] if at else r for r in (src[i], held[i], dst[i]))
+        come.append(pltpu.make_async_copy(s, h, sem.at[j]))
+        go.append(pltpu.make_async_copy(h, d, sem.at[len(parts) + j]))
+    for c in come:
+        c.start()
+    for c, g in zip(come, go):
+        c.wait()
+        g.start()
+    for g in go:
+        g.wait()
 
 
 def body(
@@ -503,7 +514,7 @@
         out_shape=[s(o.shape, o.dtype) for o in outs],
         in_specs=[hbm] * len(outs),
         out_specs=[hbm] * len(outs),
-        scratch_shapes=[v(o.shape, o.dtype) for o in outs] + [pltpu.SemaphoreType.DMA((2 * len(outs),))],
+        scratch_shapes=[v(o.shape, o.dtype) for o in outs] + [pltpu.SemaphoreType.DMA((2 * sum(len(pieces(o.shape)) for o in outs),))],
         compiler_params=pltpu.CompilerParams(vmem_limit_bytes=VMEM),
     )(*outs)
     return (

time: 67.8 us -> 67.7 us (level)
  no operation moved by 1% of the time
where the time goes in v3:
time: 67.7 us; the launch traced here: 67.5 us
  Pallas kernels  66.2 us (98%)
  between operations  1.29 us (2%)
    pallas_call x1, Pallas kernels, body(): pl.pallas_call(functools.partial(kernel, factor), name='sparse_arch', out...  63.8 us
    pallas_call x1, Pallas kernels, body(): pl.pallas_call(store, name='store', out_shape=[s(o.shape, o.dtype) for o...  2.46 us

profile of v3, /device:TPU:16, one launch (start us, length us, event | category | flops | bytes accessed | tf_op | source)
XLA Modules:
  0.0 67.5 jit_solution(6879678176279823031)
XLA Ops:
  1.3 63.8 %sparse_arch.1 = (bf16[32,512]{1,0:T(8,128)(2,1)}, bf16[2,1,64,2048]{3,2,1,0:T(8,128)(2,1)}, bf16[1,1,4096,128]{3,2,1,0:T(8,128)(2,1)}, f32[2,8,64]{2,1,0:T(8,128)}, f32[1,16,128]{2,1,0:T(8,128)}) custom-call(bf16[2,1,64,2048]{3,2,1,0:T(8,128)(2,1)} %bitcast.4, s32[2,1,512]{2,1,0:T(1,128)} %wl_h.1, bf16[1,1,4096,128]{3,2,1,0:T(8,128)(2,1)} %nr_h.1, ...), custom_call_target="tpu_custom_call" | custom-call | tf_op jit(solution)/shard_map/sparse_arch/pallas_call | solution.py:494
  65.0 2.5 %store.1 = (bf16[32,512]{1,0:T(8,128)(2,1)}, bf16[2,1,64,2048]{3,2,1,0:T(8,128)(2,1)}, bf16[1,1,4096,128]{3,2,1,0:T(8,128)(2,1)}, f32[2,8,64]{2,1,0:T(8,128)}, f32[1,16,128]{2,1,0:T(8,128)}) custom-call(bf16[32,512]{1,0:T(8,128)(2,1)} %get-tuple-element.15.refs_0_, bf16[2,1,64,2048]{3,2,1,0:T(8,128)(2,1)} %get-tuple-element.16.refs_1_, ...), custom_call_target="tpu_custom_call" | custom-call | tf_op jit(solution)/shard_map/store/pallas_call | solution.py:511
